TPU v7x, 32 devices: a whole 2x2x4 slice. The times are simulated.
32 devices in a mesh: ctx: 32 (over z, y, x, core), ch: 1.
Axes of the slice: x: 2, y: 2, z: 4, core: 2. Of those that a mesh axis runs over, the one named last changes fastest.
Arguments:
- query_branch: bfloat16 [8192, 2048], P('ctx', 'ch'), may hold values from -6 to 6
- key_branch: bfloat16 [8192, 2048], P('ctx', 'ch'), may hold values from -6 to 6
- value_branch: bfloat16 [8192, 2048], P('ctx', 'ch'), may hold values from -6 to 6
- grad_output: bfloat16 [8192, 2048], P('ctx', 'ch'), may hold values from -6 to 6
- conv_output: bfloat16 [8192, 2048], P('ctx', 'ch'), may hold values from -6 to 6
- filters: float32 [8192, 512], P('ctx'), may hold values from -0.09375 to 0.09375
- genome_blocks: int32 [4], replicated, may hold values from 1 to 16, 32 in all
Outputs:
- grad_query: bfloat16 [8192, 2048], P('ctx', 'ch')
- grad_key: bfloat16 [8192, 2048], P('ctx', 'ch')
- grad_value: bfloat16 [8192, 2048], P('ctx', 'ch')
- grad_filters: float32 [8192, 512], P('ctx', 'ch')
Inputs may be any that keep to these rules, and one draw needn't show every extreme that they name: `genome_blocks`: the genomes lie in order and fill the row; the longest covers exactly 16 shards.
All inputs are finite; a program needn't handle non-finite values.
Results may differ from a plain program's by a relative error of at most 0.001.
Values sent between devices are 32-bit elements; how exact they have to be, the bound alone decides.
A program may use at most 128 MiB of HBM per device.

v0:
```python
import functools

import jax
import jax.numpy as jnp
from jax import lax
from jax.experimental import pallas as pl
from jax.experimental.pallas import tpu as pltpu
from jax.sharding import PartitionSpec as P

HALF = 128
GROUP = 8
PART = 2
UNROLL = 4
NT = (((1,), (1,)), ((), ()))


def split_bf16(x):
    high = x.astype(jnp.bfloat16)
    low = (x - high.astype(jnp.float32)).astype(jnp.bfloat16)
    return high, low


def make_masks(genomes, masks):
    lags, rows = masks.shape[:2]
    row = lax.broadcasted_iota(jnp.int32, (rows, HALF), 0)

    def owner(place):
        block = lax.shift_right_logical(place, 3)
        found = jnp.zeros((rows, HALF), jnp.int32)
        end = 0
        for g in range(genomes.shape[0]):
            end = end + genomes[g]
            found = found + jnp.where(block >= end, 1, 0)
        return found

    own = owner(row)

    def one(lag, _):
        same = owner(row + 4 * lag) == own
        masks[lag] = jnp.where(same, 1.0, 0.0).astype(jnp.bfloat16)
        return 0

    lax.fori_loop(0, lags, one, 0)


def conv_one(
    f, masks, recv, filter_in, back_out, lag_out,
    base, shift_high, shift_low, weights, accum, low_sum, high_sum,
):
    n = recv.shape[0]
    rows = GROUP * n
    pairs = filter_in.shape[0]
    lane = lax.broadcasted_iota(jnp.int32, (GROUP, HALF), 1)
    place = lax.broadcasted_iota(jnp.int32, (GROUP, HALF), 0)

    base[:rows] = recv[:, f, 0].reshape(rows, HALF)
    for move in range(4):
        high, low = split_bf16(base[4 * move:4 * move + rows])
        shift_high[move, :rows] = high
        shift_low[move, :rows] = low

    def build(c, before):
        for pair in range(UNROLL):
            for side in range(2):
                row = filter_in[c * UNROLL + pair, f, side]
                first = pltpu.roll(
                    jnp.broadcast_to(row, (GROUP, HALF)), 1, 1, stride=1, stride_axis=0
                )
                turned = [first] + [
                    pltpu.roll(first, GROUP * p, 1) for p in range(1, HALF // GROUP)
                ]
                tile = jnp.concatenate(
                    [
                        jnp.where(lane <= place + GROUP * p, turned[p], before[p])
                        for p in range(HALF // GROUP)
                    ],
                    axis=0,
                )
                high, low = split_bf16(tile)
                at = pair * 2 * HALF + side * HALF
                weights[c, at:at + HALF, :HALF] = high
                weights[c, at:at + HALF, HALF:] = low
                before = turned
        return before

    lax.fori_loop(
        0, pairs // UNROLL, build, [jnp.zeros((GROUP, HALF), jnp.float32)] * (HALF // GROUP)
    )

    swap = (
        lax.broadcasted_iota(jnp.int32, (HALF, HALF), 1)
        + lax.broadcasted_iota(jnp.int32, (HALF, HALF), 0)
        == HALF - 1
    ).astype(jnp.bfloat16)
    gated_high, gated_low = split_bf16(recv[:, f, 1].reshape(rows, HALF))
    turned_high = lax.dot_general(
        swap, gated_high, NT, preferred_element_type=jnp.float32
    ).astype(jnp.bfloat16)
    turned_low = lax.dot_general(
        swap, gated_low, NT, preferred_element_type=jnp.float32
    ).astype(jnp.bfloat16)
    turned_both = jnp.concatenate([turned_high, turned_low], axis=0)

    accum[...] = jnp.zeros_like(accum)

    def lag_group(c, _):
        highs, lows = [], []
        for e in range(2 * UNROLL):
            lag = 2 * UNROLL * c + e
            window = pl.ds(pl.multiple_of((2 * UNROLL * c + e - e % 4) * 4, 16), rows)
            mask = masks[lag]
            highs.append(shift_high[e % 4, window] * mask)
            lows.append(shift_low[e % 4, window] * mask)
        high = jnp.concatenate(highs, axis=1)
        low = jnp.concatenate(lows, axis=1)
        accum[...] += jnp.dot(high, weights[c], preferred_element_type=jnp.float32)
        accum[:, :HALF] += jnp.dot(
            low, weights[c, :, :HALF], preferred_element_type=jnp.float32
        )
        both = jnp.dot(turned_both, high, preferred_element_type=jnp.float32)
        outer = (
            both[:HALF] + both[HALF:] + jnp.dot(turned_high, low, preferred_element_type=jnp.float32)
        )
        for side in range(2 * UNROLL):
            here = jnp.zeros((GROUP, HALF), jnp.float32)
            prior = jnp.zeros((GROUP, HALF), jnp.float32)
            for p in range(HALF // GROUP):
                part = outer[GROUP * p:GROUP * p + GROUP, side * HALF:(side + 1) * HALF]
                part = pltpu.roll(part, GROUP * p + 1, 1)
                inside = lane <= GROUP * p
                here = here + jnp.where(inside, part, 0.0)
                prior = prior + jnp.where(inside, 0.0, part)
            here = pltpu.roll(here, 0, 1, stride=1, stride_axis=0)
            prior = pltpu.roll(prior, 0, 1, stride=1, stride_axis=0)
            wrapped = lane < place
            high_sum[2 * UNROLL * c + side] = here + jnp.where(wrapped, prior, 0.0)
            low_sum[2 * UNROLL * c + side] = jnp.where(wrapped, 0.0, prior)
        return 0

    lax.fori_loop(0, pairs // UNROLL, lag_group, 0)
    total = accum[:, :HALF] + accum[:, HALF:]
    back_out[:, f] = total.reshape(n, GROUP, HALF)
    lags = jnp.sum(high_sum[...] + low_sum[1:], axis=1, keepdims=True)
    lag_out[:, :, f] = lags.reshape(pairs, 2, 1, HALF)


def spread_product(first, second, sig, send_rows, repeats):
    channels = first.shape[1]
    width = channels // repeats
    for half in range(2):
        for start in range(0, channels, HALF):
            at = (slice(half * HALF, (half + 1) * HALF), slice(start, start + HALF))
            product = first[at].astype(jnp.float32) * second[at].astype(jnp.float32)
            turn, column = start // width, start % width
            row = column * 2 * GROUP + sig * GROUP + half * 4 + turn
            send_rows[pl.ds(row, HALF, stride=2 * GROUP)] = product.T


def fused_kernel(
    repeats, genomes, query, key, value, grad, filter_send,
    grad_query, grad_key, lag_in,
    send, recv, back_in, filter_in, back_out, lag_out,
    masks, base, shift_high, shift_low, weights, accum, low_sum, high_sum,
    filter_sems, lag_sems, out_sems, in_sems, back_out_sems, back_in_sems,
):
    n, own = filter_send.shape[:2]
    pairs = filter_in.shape[0]
    pieces = own // PART
    me = lax.axis_index("ctx")

    def partner(i):
        return lax.rem(me + i, n)

    def copy(source, target, send_sem, recv_sem, device):
        return pltpu.make_async_remote_copy(
            src_ref=source, dst_ref=target, send_sem=send_sem, recv_sem=recv_sem,
            device_id={"ctx": device}, device_id_type=pl.DeviceIdType.MESH,
        )

    def each_partner(act):
        def step(i, _):
            act(partner(i))
            return 0

        lax.fori_loop(1, n, step, 0)

    def chosen(piece):
        return pl.ds(piece * PART, PART)

    def sent(other, piece):
        count = PART * 2 * GROUP
        start = pl.multiple_of(other * (own * 2 * GROUP) + piece * count, count)
        return send.at[pl.ds(start, count)].reshape(PART, 2, GROUP, HALF)

    def returned(piece):
        count = PART * GROUP
        start = pl.multiple_of(me * (own * GROUP) + piece * count, count)
        return back_in.at[pl.ds(start, count)].reshape(PART, GROUP, HALF)

    def waiter(ref, send_sem, recv_sem):
        return copy(ref, ref, send_sem, recv_sem, partner(1))

    barrier = pltpu.get_barrier_semaphore()
    each_partner(
        lambda other: pl.semaphore_signal(
            barrier, inc=1, device_id={"ctx": other}, device_id_type=pl.DeviceIdType.MESH
        )
    )
    pl.semaphore_wait(barrier, n - 1)

    @pl.when(me < pairs)
    def _():
        each_partner(
            lambda other: copy(
                filter_send.at[other], filter_in.at[me], filter_sems.at[0], filter_sems.at[1], other
            ).start()
        )

    if repeats < 4:
        send[...] = jnp.zeros_like(send)
    spread_product(grad, value, 0, send, repeats)
    spread_product(query, key, 1, send, repeats)

    def send_piece(piece, _):
        each_partner(
            lambda other: copy(
                sent(other, piece), recv.at[me, chosen(piece)],
                out_sems.at[piece], in_sems.at[piece], other,
            ).start()
        )
        return 0

    lax.fori_loop(0, pieces, send_piece, 0)

    mine = send[pl.ds(pl.multiple_of(me * (own * 2 * GROUP), 16), own * 2 * GROUP)]
    recv[me] = mine.reshape(own, 2, GROUP, HALF)
    make_masks(genomes, masks)
    base[...] = jnp.zeros_like(base)
    shift_high[...] = jnp.zeros_like(shift_high)
    shift_low[...] = jnp.zeros_like(shift_low)
    low_sum[2 * pairs] = jnp.zeros((GROUP, HALF), jnp.float32)

    @pl.when(me < pairs)
    def _():
        filter_in[me] = filter_send[me]
        waiter(filter_in.at[pl.ds(0, pairs - 1)], filter_sems.at[0], filter_sems.at[1]).wait_recv()

    @pl.when(me >= pairs)
    def _():
        waiter(filter_in, filter_sems.at[0], filter_sems.at[1]).wait_recv()

    def work(piece, _):
        waiter(
            recv.at[pl.ds(0, n - 1), chosen(piece)], out_sems.at[piece], in_sems.at[piece]
        ).wait_recv()

        def one(i, _):
            conv_one(
                piece * PART + i, masks, recv, filter_in, back_out, lag_out,
                base, shift_high, shift_low, weights, accum, low_sum, high_sum,
            )
            return 0

        lax.fori_loop(0, PART, one, 0)
        each_partner(
            lambda other: copy(
                back_out.at[other, chosen(piece)], returned(piece),
                back_out_sems.at[piece], back_in_sems.at[piece], other,
            ).start()
        )
        start = pl.multiple_of(me * (own * GROUP) + piece * (PART * GROUP), PART * GROUP)
        back_in[pl.ds(start, PART * GROUP)] = back_out[me, chosen(piece)].reshape(
            PART * GROUP, HALF
        )

        def send_lags(other, _):
            @pl.when(other != me)
            def _():
                copy(
                    lag_out.at[other, :, chosen(piece)], lag_in.at[me, :, chosen(piece)],
                    lag_sems.at[0], lag_sems.at[1], other,
                ).start()

            return 0

        lax.fori_loop(0, pairs, send_lags, 0)
        return 0

    lax.fori_loop(0, pieces, work, 0)

    @pl.when(me < pairs)
    def _():
        lag_in[me] = lag_out[me]
        waiter(filter_send.at[pl.ds(0, n - 1)], filter_sems.at[0], filter_sems.at[1]).wait_send()
        waiter(lag_out.at[pl.ds(0, pairs - 1)], lag_sems.at[0], lag_sems.at[1]).wait_send()
        waiter(lag_in.at[pl.ds(0, n - 1)], lag_sems.at[0], lag_sems.at[1]).wait_recv()

    @pl.when(me >= pairs)
    def _():
        lag_in[...] = jnp.zeros_like(lag_in)
        waiter(lag_out, lag_sems.at[0], lag_sems.at[1]).wait_send()

    def finish(piece, _):
        waiter(
            recv.at[pl.ds(0, n - 1), chosen(piece)], out_sems.at[piece], in_sems.at[piece]
        ).wait_send()
        waiter(
            back_out.at[pl.ds(0, n - 1), chosen(piece)], back_out_sems.at[piece],
            back_in_sems.at[piece],
        ).wait()
        return 0

    lax.fori_loop(0, pieces, finish, 0)
    channels = query.shape[1]
    width = channels // repeats
    for half in range(2):
        for start in range(0, channels, HALF):
            at = (slice(half * HALF, (half + 1) * HALF), slice(start, start + HALF))
            row = start % width * GROUP + half * 4 + start // width
            back = back_in[pl.ds(row, HALF, stride=GROUP)].T
            grad_query[at] = (back * key[at].astype(jnp.float32)).astype(jnp.bfloat16)
            grad_key[at] = (back * query[at].astype(jnp.float32)).astype(jnp.bfloat16)


def convolve(genomes, query, key, value, grad, filters):
    n, own = filters.shape[:2]
    pairs = n // 2
    pieces = own // PART
    rows = GROUP * n
    padded = rows + 4 * n
    repeats = query.shape[1] // (n * own)
    signals = (n, own, 2, GROUP, HALF)
    vmem = pl.BlockSpec(memory_space=pltpu.VMEM)
    flops = own * 2 * pairs * 2 * rows * 256 * (256 + 128 + 192)
    return pl.pallas_call(
        functools.partial(fused_kernel, repeats),
        in_specs=[pl.BlockSpec(memory_space=pltpu.SMEM)] + [vmem] * 5,
        out_specs=[vmem] * 3,
        out_shape=[
            jax.ShapeDtypeStruct(query.shape, jnp.bfloat16),
            jax.ShapeDtypeStruct(query.shape, jnp.bfloat16),
            jax.ShapeDtypeStruct((n, 2, own, 1, HALF), jnp.float32),
        ],
        scratch_shapes=[
            pltpu.VMEM((n * own * 2 * GROUP, HALF), jnp.float32),
            pltpu.VMEM(signals, jnp.float32),
            pltpu.VMEM((n * own * GROUP, HALF), jnp.float32),
            pltpu.VMEM((pairs, own, 2, 1, HALF), jnp.float32),
            pltpu.VMEM((n, own, GROUP, HALF), jnp.float32),
            pltpu.VMEM((pairs, 2, own, 1, HALF), jnp.float32),
            pltpu.VMEM((n, rows, HALF), jnp.bfloat16),
            pltpu.VMEM((rows + 16, HALF), jnp.float32),
            pltpu.VMEM((4, padded, HALF), jnp.bfloat16),
            pltpu.VMEM((4, padded, HALF), jnp.bfloat16),
            pltpu.VMEM((pairs // UNROLL, 256 * UNROLL, 256), jnp.bfloat16),
            pltpu.VMEM((rows, 256), jnp.float32),
            pltpu.VMEM((2 * pairs + 1, GROUP, HALF), jnp.float32),
            pltpu.VMEM((2 * pairs, GROUP, HALF), jnp.float32),
            pltpu.SemaphoreType.DMA((2,)),
            pltpu.SemaphoreType.DMA((2,)),
            pltpu.SemaphoreType.DMA((pieces,)),
            pltpu.SemaphoreType.DMA((pieces,)),
            pltpu.SemaphoreType.DMA((pieces,)),
            pltpu.SemaphoreType.DMA((pieces,)),
        ],
        compiler_params=pltpu.CompilerParams(
            collective_id=0, has_side_effects=True, vmem_limit_bytes=52 * 1024 * 1024
        ),
        cost_estimate=pl.CostEstimate(
            flops=flops, bytes_accessed=5 * query.size * 2, transcendentals=0
        ),
    )(genomes, query, key, value, grad, filters)


def local(query_branch, key_branch, value_branch, grad_output, conv_output, filters, genome_blocks):
    rows, channels = query_branch.shape
    width = filters.shape[1]
    blocks = lax.axis_size("ctx")
    own = width // blocks
    grad_value = (grad_output.astype(jnp.float32) * conv_output.astype(jnp.float32)).astype(
        jnp.bfloat16
    )
    filter_parts = filters.reshape(2, HALF, blocks, own)[:, ::-1].transpose(2, 3, 0, 1)
    grad_query, grad_key, lag = convolve(
        genome_blocks, query_branch, key_branch, value_branch, grad_output,
        filter_parts[:, :, :, None],
    )
    lag = lag[:, :, :, 0].transpose(1, 3, 0, 2).reshape(rows, width)
    scaled = lag * (rows * blocks) ** (-0.5)
    grad_filters = lax.psum_scatter(scaled, "ch", scatter_dimension=1, tiled=True)
    return (grad_query, grad_key, grad_value, grad_filters)


def solution(mesh):
    in_specs = (
        P("ctx", "ch"),
        P("ctx", "ch"),
        P("ctx", "ch"),
        P("ctx", "ch"),
        P("ctx", "ch"),
        P("ctx", None),
        P(),
    )
    out_specs = (P("ctx", "ch"), P("ctx", "ch"), P("ctx", "ch"), P("ctx", "ch"))
    return jax.shard_map(local, mesh=mesh, in_specs=in_specs, out_specs=out_specs, check_vma=False)
```

profile of v0, /device:TPU:0, one launch (start us, length us, event | category | flops | bytes accessed | tf_op | source)
XLA Modules:
  0.0 171.5 jit_solution(18054682957679573766)
XLA Ops:
  0.6 1.2 copy.12
  1.9 0.0 copy-start
  1.9 0.3 reshape.16
  2.2 1.2 rev.3
  3.4 0.0 copy-done
  3.4 161.6 %shard_map.102 = (bf16[256,2048]{1,0:T(8,128)(2,1)}, bf16[256,2048]{1,0:T(8,128)(2,1)}, f32[32,2,16,1,128]{4,3,2,1,0:T(1,128)S(1)}) custom-call(s32[4]{0:T(128)S(1)} %copy-done, bf16[256,2048]{1,0:T(8,128)(2,1)} %query.1, bf16[256,2048]{1,0:T(8,128)(2,1)} %key.1, bf16[256,2048]{1,0:T(8,128)(2,1)} %value.1, bf16[256,2048]{1,0:T(8,128)(2,1)} %grad.1, ...), custom_call_target="tpu_custom_call" | custom-call | flops 38654705664 | bytes 5242880 | tf_op jit(solution)/shard_map/pallas_call | solution.py:335
  165.0 0.6 broadcast_multiply_fusion
  165.6 0.3 copy.13
  165.9 0.0 copy-start.1
  165.9 0.0 copy-start.2
  165.9 1.0 copy.14
  166.9 0.2 copy-done.1
  167.2 0.4 copy-done.2
  167.6 0.0 copy-start.4
  167.6 1.4 multiply_convert_fusion
  169.0 0.0 copy-done.4
  169.0 0.0 copy-start.3
  169.0 1.0 copy.20
  169.9 0.6 copy-done.3
  170.6 1.0 copy.21
  (1 shorter events, 0.0 us)
Async XLA Ops:
  1.9 1.5 copy-start
  165.9 1.3 copy-start.1
  165.9 1.7 %copy-start.2 = (bf16[256,2048]{1,0:T(8,128)(2,1)S(1)}, bf16[256,2048]{1,0:T(8,128)(2,1)}, u32[]{:S(2)}) copy-start(bf16[256,2048]{1,0:T(8,128)(2,1)} %param.11) | copy-start | bytes 3145732
  167.6 1.4 copy-start.4
  169.0 1.6 copy-start.3
where the time goes:
time: 172 us
  Pallas kernels  162 us (94%)
  local copies, waits for them, and re-layouts  7.3 us (4%)
  other arithmetic  1.95 us (1%)
    pallas_call x1, Pallas kernels, convolve(): pl.pallas_call(functools.partial(fused_kernel, repeats), in_specs=[pl.Blo...  162 us
    unnamed x15, local copies, waits for them, and re-layouts  5.53 us

commit v1 on v0

--- a/solution.py
+++ b/solution.py
@@ -11,6 +11,8 @@
 GROUP = 8
 PART = 2
 UNROLL = 4
+STRIDE = 13
+EARLY = 2
 NT = (((1,), (1,)), ((), ()))
 
 
@@ -169,7 +171,7 @@
     me = lax.axis_index("ctx")
 
     def partner(i):
-        return lax.rem(me + i, n)
+        return lax.rem(me + STRIDE * i, n)
 
     def copy(source, target, send_sem, recv_sem, device):
         return pltpu.make_async_remote_copy(
@@ -218,8 +220,18 @@
 
     if repeats < 4:
         send[...] = jnp.zeros_like(send)
-    spread_product(grad, value, 0, send, repeats)
-    spread_product(query, key, 1, send, repeats)
+
+    def send_half(sig):
+        def one(piece, _):
+            each_partner(
+                lambda other: copy(
+                    sent(other, piece).at[:, sig], recv.at[me, chosen(piece), sig],
+                    out_sems.at[piece], in_sems.at[piece], other,
+                ).start()
+            )
+            return 0
+
+        lax.fori_loop(0, EARLY, one, 0)
 
     def send_piece(piece, _):
         each_partner(
@@ -230,7 +242,11 @@
         )
         return 0
 
-    lax.fori_loop(0, pieces, send_piece, 0)
+    spread_product(grad, value, 0, send, repeats)
+    send_half(0)
+    spread_product(query, key, 1, send, repeats)
+    send_half(1)
+    lax.fori_loop(EARLY, pieces, send_piece, 0)
 
     mine = send[pl.ds(pl.multiple_of(me * (own * 2 * GROUP), 16), own * 2 * GROUP)]
     recv[me] = mine.reshape(own, 2, GROUP, HALF)

time: 172 us -> 171 us (level)
  Pallas kernels: 162 us -> 160 us
where the time goes in v1:
time: 171 us; the launch traced here: 170 us
  Pallas kernels  160 us (94%)
  local copies, waits for them, and re-layouts  7.3 us (4%)
  other arithmetic  1.95 us (1%)
    pallas_call x1, Pallas kernels, convolve(): pl.pallas_call(functools.partial(fused_kernel, repeats), in_specs=[pl.Blo...  160 us
    unnamed x15, local copies, waits for them, and re-layouts  5.53 us

profile of v1, /device:TPU:0, one launch (start us, length us, event | category | flops | bytes accessed | tf_op | source)
XLA Modules:
  0.0 170.3 jit_solution(17216315484532047505)
XLA Ops:
  0.6 1.2 copy.12
  1.9 0.0 copy-start
  1.9 0.3 reshape.16
  2.2 1.2 rev.3
  3.4 0.0 copy-done
  3.4 160.3 %shard_map.102 = (bf16[256,2048]{1,0:T(8,128)(2,1)}, bf16[256,2048]{1,0:T(8,128)(2,1)}, f32[32,2,16,1,128]{4,3,2,1,0:T(1,128)S(1)}) custom-call(s32[4]{0:T(128)S(1)} %copy-done, bf16[256,2048]{1,0:T(8,128)(2,1)} %query.1, bf16[256,2048]{1,0:T(8,128)(2,1)} %key.1, bf16[256,2048]{1,0:T(8,128)(2,1)} %value.1, bf16[256,2048]{1,0:T(8,128)(2,1)} %grad.1, ...), custom_call_target="tpu_custom_call" | custom-call | flops 38654705664 | bytes 5242880 | tf_op jit(solution)/shard_map/pallas_call | solution.py:351
  163.7 0.6 broadcast_multiply_fusion
  164.3 0.3 copy.13
  164.6 0.0 copy-start.1
  164.6 0.0 copy-start.2
  164.7 1.0 copy.14
  165.7 0.2 copy-done.1
  165.9 0.4 copy-done.2
  166.3 0.0 copy-start.4
  166.3 1.4 multiply_convert_fusion
  167.7 0.0 copy-done.4
  167.7 0.0 copy-start.3
  167.7 1.0 copy.20
  168.7 0.6 copy-done.3
  169.3 1.0 copy.21
  (1 shorter events, 0.0 us)
Async XLA Ops:
  1.9 1.5 copy-start
  164.6 1.3 copy-start.1
  164.6 1.7 %copy-start.2 = (bf16[256,2048]{1,0:T(8,128)(2,1)S(1)}, bf16[256,2048]{1,0:T(8,128)(2,1)}, u32[]{:S(2)}) copy-start(bf16[256,2048]{1,0:T(8,128)(2,1)} %param.11) | copy-start | bytes 3145732
  166.3 1.4 copy-start.4
  167.7 1.6 copy-start.3

commit v2 on v1

--- a/solution.py
+++ b/solution.py
@@ -115,9 +115,8 @@
             lows.append(shift_low[e % 4, window] * mask)
         high = jnp.concatenate(highs, axis=1)
         low = jnp.concatenate(lows, axis=1)
-        accum[...] += jnp.dot(high, weights[c], preferred_element_type=jnp.float32)
-        accum[:, :HALF] += jnp.dot(
-            low, weights[c, :, :HALF], preferred_element_type=jnp.float32
+        accum[...] += jnp.dot(
+            jnp.concatenate([high, low], axis=0), weights[c], preferred_element_type=jnp.float32
         )
         both = jnp.dot(turned_both, high, preferred_element_type=jnp.float32)
         outer = (
@@ -140,7 +139,9 @@
         return 0
 
     lax.fori_loop(0, pairs // UNROLL, lag_group, 0)
-    total = accum[:, :HALF] + accum[:, HALF:]
+    total = (
+        accum[:rows, :HALF] + accum[:rows, HALF:] + accum[rows:, :HALF] + accum[rows:, HALF:]
+    )
     back_out[:, f] = total.reshape(n, GROUP, HALF)
     lags = jnp.sum(high_sum[...] + low_sum[1:], axis=1, keepdims=True)
     lag_out[:, :, f] = lags.reshape(pairs, 2, 1, HALF)
@@ -369,7 +370,7 @@
             pltpu.VMEM((4, padded, HALF), jnp.bfloat16),
             pltpu.VMEM((4, padded, HALF), jnp.bfloat16),
             pltpu.VMEM((pairs // UNROLL, 256 * UNROLL, 256), jnp.bfloat16),
-            pltpu.VMEM((rows, 256), jnp.float32),
+            pltpu.VMEM((2 * rows, 256), jnp.float32),
             pltpu.VMEM((2 * pairs + 1, GROUP, HALF), jnp.float32),
             pltpu.VMEM((2 * pairs, GROUP, HALF), jnp.float32),
             pltpu.SemaphoreType.DMA((2,)),

time: 171 us -> 170 us (level)
  no operation moved by 1% of the time
where the time goes in v2:
time: 170 us
  Pallas kernels  160 us (94%)
  local copies, waits for them, and re-layouts  7.3 us (4%)
  other arithmetic  1.95 us (1%)
    pallas_call x1, Pallas kernels, convolve(): pl.pallas_call(functools.partial(fused_kernel, repeats), in_specs=[pl.Blo...  160 us
    unnamed x15, local copies, waits for them, and re-layouts  5.53 us

profile of v2, /device:TPU:0, one launch (start us, length us, event | category | flops | bytes accessed | tf_op | source)
XLA Modules:
  0.0 170.2 jit_solution(3030585089486277085)
XLA Ops:
  0.6 1.2 copy.12
  1.9 0.0 copy-start
  1.9 0.3 reshape.16
  2.2 1.2 rev.3
  3.4 0.0 copy-done
  3.4 160.3 %shard_map.102 = (bf16[256,2048]{1,0:T(8,128)(2,1)}, bf16[256,2048]{1,0:T(8,128)(2,1)}, f32[32,2,16,1,128]{4,3,2,1,0:T(1,128)S(1)}) custom-call(s32[4]{0:T(128)S(1)} %copy-done, bf16[256,2048]{1,0:T(8,128)(2,1)} %query.1, bf16[256,2048]{1,0:T(8,128)(2,1)} %key.1, bf16[256,2048]{1,0:T(8,128)(2,1)} %value.1, bf16[256,2048]{1,0:T(8,128)(2,1)} %grad.1, ...), custom_call_target="tpu_custom_call" | custom-call | flops 38654705664 | bytes 5242880 | tf_op jit(solution)/shard_map/pallas_call | solution.py:352
  163.7 0.6 broadcast_multiply_fusion
  164.3 0.3 copy.13
  164.5 0.0 copy-start.1
  164.6 0.0 copy-start.2
  164.6 1.0 copy.14
  165.6 0.2 copy-done.1
  165.8 0.4 copy-done.2
  166.3 0.0 copy-start.4
  166.3 1.4 multiply_convert_fusion
  167.6 0.0 copy-done.4
  167.6 0.0 copy-start.3
  167.7 1.0 copy.20
  168.6 0.6 copy-done.3
  169.3 1.0 copy.21
  (1 shorter events, 0.0 us)
Async XLA Ops:
  1.9 1.5 copy-start
  164.5 1.3 copy-start.1
  164.6 1.7 %copy-start.2 = (bf16[256,2048]{1,0:T(8,128)(2,1)S(1)}, bf16[256,2048]{1,0:T(8,128)(2,1)}, u32[]{:S(2)}) copy-start(bf16[256,2048]{1,0:T(8,128)(2,1)} %param.11) | copy-start | bytes 3145732
  166.3 1.4 copy-start.4
  167.6 1.6 copy-start.3

commit v3 on v2

--- a/solution.py
+++ b/solution.py
@@ -9,10 +9,10 @@
 
 HALF = 128
 GROUP = 8
-PART = 2
+PART = 4
 UNROLL = 4
 STRIDE = 13
-EARLY = 2
+EARLY = 1
 NT = (((1,), (1,)), ((), ()))
 
 

time: 170 us -> 180 us (1.059)
  Pallas kernels: 160 us -> 170 us
    pallas_call x1, Pallas kernels: 160 us -> 170 us  [convolve(): pl.pallas_call(functools.partial(fused_kernel, repeats), in_specs=[pl.Blo...]
where the time goes in v3:
time: 180 us
  Pallas kernels  170 us (94%)
  local copies, waits for them, and re-layouts  7.3 us (4%)
  other arithmetic  1.95 us (1%)
    pallas_call x1, Pallas kernels, convolve(): pl.pallas_call(functools.partial(fused_kernel, repeats), in_specs=[pl.Blo...  170 us
    unnamed x15, local copies, waits for them, and re-layouts  5.53 us

profile of v3, /device:TPU:0, one launch (start us, length us, event | category | flops | bytes accessed | tf_op | source)
XLA Modules:
  0.0 179.6 jit_solution(904951455795804784)
XLA Ops:
  0.6 1.2 copy.12
  1.9 0.0 copy-start
  1.9 0.3 reshape.16
  2.2 1.2 rev.3
  3.4 0.0 copy-done
  3.4 169.6 %shard_map.102 = (bf16[256,2048]{1,0:T(8,128)(2,1)}, bf16[256,2048]{1,0:T(8,128)(2,1)}, f32[32,2,16,1,128]{4,3,2,1,0:T(1,128)S(1)}) custom-call(s32[4]{0:T(128)S(1)} %copy-done, bf16[256,2048]{1,0:T(8,128)(2,1)} %query.1, bf16[256,2048]{1,0:T(8,128)(2,1)} %key.1, bf16[256,2048]{1,0:T(8,128)(2,1)} %value.1, bf16[256,2048]{1,0:T(8,128)(2,1)} %grad.1, ...), custom_call_target="tpu_custom_call" | custom-call | flops 38654705664 | bytes 5242880 | tf_op jit(solution)/shard_map/pallas_call | solution.py:352
  173.0 0.6 broadcast_multiply_fusion
  173.6 0.3 copy.13
  173.9 0.0 copy-start.1
  173.9 0.0 copy-start.2
  174.0 1.0 copy.14
  175.0 0.2 copy-done.1
  175.2 0.4 copy-done.2
  175.6 0.0 copy-start.4
  175.6 1.4 multiply_convert_fusion
  177.0 0.0 copy-done.4
  177.0 0.0 copy-start.3
  177.0 1.0 copy.20
  178.0 0.6 copy-done.3
  178.6 1.0 copy.21
  (1 shorter events, 0.0 us)
Async XLA Ops:
  1.9 1.5 copy-start
  173.9 1.3 copy-start.1
  173.9 1.7 copy-start.2
  175.6 1.4 copy-start.4
  177.0 1.6 copy-start.3
